TPU v7x, 256 devices: a whole 4x4x8 slice. The times are simulated.
256 devices in a mesh: dp: 8 (over y_hi, x), cent: 32 (over z, y_lo, core).
Axes of the slice: x: 4, y: 4 (y_hi: 2, y_lo: 2; y = y_hi * 2 + y_lo), z: 8, core: 2. Of those that a mesh axis runs over, the one named last changes fastest.
Arguments:
- minibatch: bfloat16 [16384, 768], P(('dp', 'cent')), may hold values from -80 to 80
- centroids: float32 [32768, 768], P('cent'), may hold values from -40 to 40
Outputs:
- refined: float32 [32768, 768], P('cent')
- log_partition: float32 [16384], P('dp')
All inputs are finite; a program needn't handle non-finite values.
Results may differ from a plain program's by a relative error of at most 0.0013.
Values may be sent and summed in bfloat16 or wider, within the bound.
A program may use at most 64 MiB of HBM per device.

v0:
```python
import jax
import jax.numpy as jnp
from jax import lax
from jax.sharding import PartitionSpec as P

ITERS = 2


INV_TEMP = 20.0
PRIOR = 0.5
EPS = 1e-06


def rms_unit(values):
    wide = values.astype(jnp.float32)
    return wide * lax.rsqrt(jnp.mean(wide * wide, axis=-1, keepdims=True) + EPS)


def row_scores(rows, center_bf, factor):
    scores = (
        lax.dot_general(
            rows, center_bf, (((1,), (1,)), ((), ())), preferred_element_type=jnp.float32
        )
        * factor
    )
    expo = jnp.exp(scores - INV_TEMP)
    return (expo, jnp.sum(expo, axis=1))


def weighted(expo, total, rows):
    probs = (expo / total[:, None]).astype(jnp.bfloat16)
    numer = lax.dot_general(
        probs, rows, (((0,), (0,)), ((), ())), preferred_element_type=jnp.float32
    )
    mass = jnp.sum(probs, axis=0, dtype=jnp.float32)
    return (numer, mass)


def on_device(minibatch, centroids):
    unit_rows = lax.all_gather(rms_unit(minibatch).astype(jnp.bfloat16), "cent", axis=0, tiled=True)
    factor = INV_TEMP / unit_rows.shape[1]
    centers = rms_unit(centroids)
    center_bf = centers.astype(jnp.bfloat16)
    total = jnp.ones((unit_rows.shape[0],), jnp.float32)
    for step in range(ITERS):
        expo, partial_value = row_scores(unit_rows, center_bf, factor)
        total = lax.psum(partial_value, "cent")
        numer, mass = weighted(expo, total, unit_rows)
        numer, mass = lax.psum((numer, mass), "dp")
        centers = (numer + PRIOR * centers) / (mass + PRIOR)[:, None]
        center_bf = centers.astype(jnp.bfloat16)
    return (centers, jnp.log(total))


def solution(mesh):
    return jax.shard_map(
        on_device,
        mesh=mesh,
        in_specs=(P(("dp", "cent"), None), P("cent", None)),
        out_specs=(P("cent", None), P("dp")),
        check_vma=False,
    )
```

profile of v0, /device:TPU:2, one launch (start us, length us, event | category | flops | bytes accessed | tf_op | source)
XLA Modules:
  0.0 444.1 jit_solution(17967588130649990453)
XLA Ops:
  7.2 0.0 copy-start
  7.2 0.0 all-gather.2.cloned.1.call-start
  7.2 1.2 fusion.6
  8.4 1.6 fusion.7
  10.0 0.0 all-gather.2.cloned.1.call-update
  10.0 0.0 all-reduce.3.cloned.1.call-start
  10.1 2.2 multiply_reduce_fusion
  12.3 67.3 %all-gather.2.cloned.1.call-done = bf16[2048,768]{1,0:T(8,128)(2,1)} async-done(((bf16[64,768]{1,0:T(8,128)(2,1)}), bf16[2048,768]{1,0:T(8,128)(2,1)}) %all-gather.2.cloned.1.call-update) | async-done | bytes 3145744 | tf_op jit(solution)/shard_map/all_gather | solution.py:40
  79.6 0.0 copy-done
  79.6 8.8 %fusion = (f32[2048]{0:T(1024)S(1)}, f32[2048,1024]{1,0:T(8,128)}) fusion(bf16[2048,768]{1,0:T(8,128)(2,1)} %all-gather.2.cloned.1.call-done, f32[1024,768]{1,0:T(8,128)S(1)} %copy-done, f32[1024]{0:T(1024)S(1)} %add_rsqrt_fusion), kind=kOutput, calls=%fused_computation.6 | convolution fusion | flops 3229087744 | bytes 14692352 | tf_op jit(solution)/shard_map/dot_general | solution.py:21
  88.3 55.5 %psum.42 = f32[2048]{0:T(1024)S(1)} all-reduce(f32[2048]{0:T(1024)S(1)} %get-tuple-element.6), channel_id=1, replica_groups=mesh['dp'=8,'cent'=32] {'cent'}, use_global_device_ids=true, to_apply=%region_3.0 | all-reduce | flops 2048 | bytes 16384 | tf_op jit(solution)/shard_map/psum | solution.py:47
  143.8 0.0 copy-start.1
  143.8 4.6 %convert_reduce_fusion.1 = (f32[1024]{0:T(1024)S(1)}, bf16[2048,1024]{1,0:T(8,128)(2,1)S(1)}) fusion(f32[2048]{0:T(1024)S(1)} %psum.42, f32[2048,1024]{1,0:T(8,128)} %get-tuple-element.7), kind=kLoop, calls=%fused_computation.3 | loop fusion | flops 12581888 | bytes 12595200 | tf_op jit(solution)/shard_map/reduce_sum | solution.py:35
  148.5 0.0 copy-done.1
  148.5 5.2 %fusion.8 = f32[1024,768]{1,0:T(8,128)} fusion(bf16[2048,1024]{1,0:T(8,128)(2,1)S(1)} %get-tuple-element.5, bf16[2048,768]{1,0:T(8,128)(2,1)S(1)} %copy-done.1), kind=kOutput, calls=%fused_computation.24 | convolution fusion | flops 3221225472 | bytes 10485760 | tf_op jit(solution)/shard_map/dot_general | solution.py:32
  153.7 0.0 all-reduce.3.cloned.1.call-update
  153.7 0.0 all-reduce.5.cloned.1.call-start
  153.7 19.9 %psum.44 = f32[1024]{0:T(1024)S(1)} all-reduce(f32[1024]{0:T(1024)S(1)} %get-tuple-element.4), channel_id=1, replica_groups=mesh['dp'=8,'cent'=32] {'dp'}, use_global_device_ids=true, to_apply=%region_6.0 | all-reduce | flops 1024 | bytes 8192 | tf_op jit(solution)/shard_map/psum | solution.py:49
  173.7 81.6 %all-reduce.3.cloned.1.call-done = f32[1024,768]{1,0:T(8,128)} async-done(((f32[1024,768]{1,0:T(8,128)}), f32[1024,768]{1,0:T(8,128)}) %all-reduce.3.cloned.1.call-update) | async-done | bytes 3145744 | tf_op jit(solution)/shard_map/psum | solution.py:49
  255.2 10.4 %fusion.1 = (f32[2048]{0:T(1024)S(1)}, f32[2048,1024]{1,0:T(8,128)}) fusion(bf16[2048,768]{1,0:T(8,128)(2,1)} %all-gather.2.cloned.1.call-done, f32[1024]{0:T(1024)S(1)} %broadcast_add_fusion.1, f32[1024,768]{1,0:T(8,128)} %all-reduce.3.cloned.1.call-done, f32[1024,768]{1,0:T(8,128)S(1)} %copy-done, f32[1024]{0:T(1024)S(1)} %add_rsqrt_fusion), kind=kOutput, calls=%fused_computation.7 | convolution fusion | flops 3231447040 | bytes 17842176 | tf_op jit(solution)/shard_map/dot_general | solution.py:21
  265.6 54.0 %psum.45 = f32[2048]{0:T(1024)S(1)} all-reduce(f32[2048]{0:T(1024)S(1)} %get-tuple-element.8), channel_id=1, replica_groups=mesh['dp'=8,'cent'=32] {'cent'}, use_global_device_ids=true, to_apply=%region_8.0 | all-reduce | flops 2048 | bytes 16384 | tf_op jit(solution)/shard_map/psum | solution.py:47
  319.7 0.0 copy-start.2
  319.7 4.6 %convert_reduce_fusion = (f32[1024]{0:T(1024)S(1)}, bf16[2048,1024]{1,0:T(8,128)(2,1)S(1)}) fusion(f32[2048]{0:T(1024)S(1)} %psum.45, f32[2048,1024]{1,0:T(8,128)} %get-tuple-element.9), kind=kLoop, calls=%fused_computation | loop fusion | flops 12581888 | bytes 12595200 | tf_op jit(solution)/shard_map/reduce_sum | solution.py:35
  324.3 0.0 copy-done.2
  324.3 5.2 %fusion.9 = f32[1024,768]{1,0:T(8,128)} fusion(bf16[2048,1024]{1,0:T(8,128)(2,1)S(1)} %get-tuple-element.3, bf16[2048,768]{1,0:T(8,128)(2,1)S(1)} %copy-done.2), kind=kOutput, calls=%fused_computation.25 | convolution fusion | flops 3221225472 | bytes 10485760 | tf_op jit(solution)/shard_map/dot_general | solution.py:32
  329.5 0.0 all-reduce.5.cloned.1.call-update
  329.5 0.6 log.3
  330.1 21.8 %psum.47 = f32[1024]{0:T(1024)S(1)} all-reduce(f32[1024]{0:T(1024)S(1)} %get-tuple-element.2), channel_id=1, replica_groups=mesh['dp'=8,'cent'=32] {'dp'}, use_global_device_ids=true, to_apply=%region_11.0 | all-reduce | flops 1024 | bytes 8192 | tf_op jit(solution)/shard_map/psum | solution.py:49
  352.0 81.1 %all-reduce.5.cloned.1.call-done = f32[1024,768]{1,0:T(8,128)} async-done(((f32[1024,768]{1,0:T(8,128)}), f32[1024,768]{1,0:T(8,128)}) %all-reduce.5.cloned.1.call-update) | async-done | bytes 3145744 | tf_op jit(solution)/shard_map/psum | solution.py:49
  433.0 4.6 %add_divide_fusion = f32[1024,768]{1,0:T(8,128)} fusion(f32[1024,768]{1,0:T(8,128)} %all-reduce.5.cloned.1.call-done, f32[1024]{0:T(1024)S(1)} %broadcast_add_fusion, f32[1024]{0:T(1024)S(1)} %broadcast_add_fusion.1, f32[1024,768]{1,0:T(8,128)} %all-reduce.3.cloned.1.call-done, f32[1024,768]{1,0:T(8,128)S(1)} %copy-done, f32[1024]{0:T(1024)S(1)} %add_rsqrt_fusion), kind=kLoop, calls=%fused_computation.8 | loop fusion | flops 5505024 | bytes 12595200 | tf_op jit(solution)/shard_map/div | solution.py:50
  (4 shorter events, 0.0 us)
Async XLA Ops:
  7.2 72.4 %copy-start = (f32[1024,768]{1,0:T(8,128)S(1)}, f32[1024,768]{1,0:T(8,128)}, u32[]{:S(2)}) copy-start(f32[1024,768]{1,0:T(8,128)} %param.3) | copy-start | bytes 9437188
  7.2 72.4 %all-gather.2.cloned.1.call-start = ((), (), s32[]{:S(2)}) async-start(), calls=%async_computation | async-start | bytes 3244032 | tf_op jit(solution)/shard_map/all_gather | solution.py:40
  10.0 245.2 %all-reduce.3.cloned.1.call-start = ((), (), s32[]{:S(2)}) async-start(), calls=%async_computation.1 | async-start | bytes 6291456 | tf_op jit(solution)/shard_map/psum | solution.py:49
  143.8 4.6 %copy-start.1 = (bf16[2048,768]{1,0:T(8,128)(2,1)S(1)}, bf16[2048,768]{1,0:T(8,128)(2,1)}, u32[]{:S(2)}) copy-start(bf16[2048,768]{1,0:T(8,128)(2,1)} %all-gather.2.cloned.1.call-done) | copy-start | bytes 9437188
  153.7 279.3 %all-reduce.5.cloned.1.call-start = ((), (), s32[]{:S(2)}) async-start(), calls=%async_computation.2 | async-start | bytes 6291456 | tf_op jit(solution)/shard_map/psum | solution.py:49
  319.7 4.6 %copy-start.2 = (bf16[2048,768]{1,0:T(8,128)(2,1)S(1)}, bf16[2048,768]{1,0:T(8,128)(2,1)}, u32[]{:S(2)}) copy-start(bf16[2048,768]{1,0:T(8,128)(2,1)} %all-gather.2.cloned.1.call-done) | copy-start | bytes 9437188
Sparse Core Ops, SparseCore 0:
  10.4 69.0 all-gather.1
  153.8 101.3 all-reduce.2
  329.6 103.3 all-reduce.4
where the time goes:
time: 446 us; the launch traced here: 444 us
  waiting for transfers between devices  230 us (52%)
  blocking collectives  151 us (34%)
  matrix products  29.5 us (7%)
  other arithmetic  18.8 us (4%)
  between operations  13.9 us (3%)
    psum x2, waiting for transfers between devices, on_device(): numer, mass = lax.psum((numer, mass), 'dp')  163 us
    psum x2, blocking collectives, on_device(): total = lax.psum(partial_value, 'cent')  110 us
    all_gather x1, waiting for transfers between devices, on_device(): lax.all_gather(rms_unit(minibatch).astype(jnp.bfloat16), 'cent', axis=0,...  67.3 us
    psum x2, blocking collectives, on_device(): numer, mass = lax.psum((numer, mass), 'dp')  41.8 us
    dot_general x2, matrix products, row_scores(): lax.dot_general(rows, center_bf, (((1,), (1,)), ((), ())), preferred_elem...  19.1 us
    dot_general x2, matrix products, weighted(): lax.dot_general(probs, rows, (((0,), (0,)), ((), ())), preferred_element_...  10.3 us
    reduce_sum x2, other arithmetic, weighted(): mass = jnp.sum(probs, axis=0, dtype=jnp.float32)  9.25 us
  transfers between devices with their start and end apart: 3, of which 3 were waited for; matrix products, arithmetic and copies ran while one was open for 1% of the time, Pallas kernels for 0%

commit v1 on v0

v1 whole, which is shorter than its diff:
```python
import functools

import jax
import jax.numpy as jnp
from jax import lax
from jax.experimental import pallas as pl
from jax.experimental.pallas import tpu as pltpu
from jax.sharding import PartitionSpec as P

MESH = pl.DeviceIdType.MESH
ITERS = 2
INV_TEMP = 20.0
PRIOR = 0.5
EPS = 1e-06
LOG2E = 1.4426950408889634
NX, NY, NZ, NC = 4, 4, 8, 2
BLOCK = 64
HALF = BLOCK // 2
CHUNK = 256
NCHUNK = 16
KC = 128
KD = NX * KC
D = 768
BF = jnp.bfloat16
F32 = jnp.float32


def encode(v):
    s = v * v
    return (v * jnp.abs(v) * s).astype(BF)


def decode(code):
    y = code.astype(F32)
    r = lax.rsqrt(jnp.maximum(jnp.abs(y), 1e-37))
    return y * (r * r * lax.rsqrt(r))


def body(
    mb, cents, out, tot_out,
    rows, cen_in, cb, c_own, expo, probs, macc, tp, ar_a, ar_b, ar_c, ar_u, tot, inv,
    num_own, sb, ms, rb, mr, coded,
    gs, gr, cs, cr, as_, ar, bs, br, zs, zr, ds_, dr, rs_s, rs_r, ms_s, ms_r, ag_s, ag_r, fs, fr, loc, os_,
):
    dp, ce = lax.axis_index("dp"), lax.axis_index("cent")
    yh, x = dp // 4, lax.rem(dp, 4)
    z, yl, c = ce // 4, lax.rem(ce, 4) // 2, lax.rem(ce, 2)
    y = yh * 2 + yl

    def dev(dy=0, dx=0, dz=0, dc=0):
        yy, xx = lax.rem(y + dy + NY, NY), lax.rem(x + dx + NX, NX)
        zz, cc = lax.rem(z + dz + NZ, NZ), lax.rem(c + dc, NC)
        return ((yy // 2) * 4 + xx, zz * 4 + lax.rem(yy, 2) * 2 + cc)

    def copy(src, dst, ss, rs, to):
        return pltpu.make_async_remote_copy(
            src_ref=src, dst_ref=dst, send_sem=ss, recv_sem=rs, device_id=to, device_id_type=MESH
        )

    peers = [dict(dc=1)]
    peers += [dict(dy=d) for d in (1, 2, 3)]
    peers += [dict(dx=d) for d in (1, 2, 3)]
    peers += [dict(dz=d) for d in range(1, NZ)]
    barrier = pltpu.get_barrier_semaphore()
    for p in peers:
        pl.semaphore_signal(barrier, inc=1, device_id=dev(**p), device_id_type=MESH)
    load = pltpu.make_async_copy(cents.at[pl.ds(yh * KD, KD)], cen_in, loc)
    load.start()

    def unit(v):
        return v * lax.rsqrt(jnp.mean(v * v, axis=-1, keepdims=True) + EPS)

    rows[yh, z, yl, c] = unit(mb[...].astype(F32)).astype(BF)
    pl.semaphore_wait(barrier, len(peers))

    def blk(dy, dz, half=None):
        yy = lax.rem(y + dy + NY, NY)
        r = rows.at[yy // 2, lax.rem(z + dz + NZ, NZ), lax.rem(yy, 2), c]
        return r if half is None else r.at[pl.ds(half * HALF, HALF)]

    def rsem(dy, dz, half=None):
        return gr.at[dy % NY, dz % NZ, half or 0]

    def lane(first_z):
        sends = []

        def send(dy, dz, ey, ez, half=None):
            cp = copy(
                blk(dy, dz, half), blk(dy, dz, half), gs.at[len(sends)],
                rsem(dy - ey, dz - ez, half), dev(dy=ey, dz=ez),
            )
            cp.start()
            sends.append(cp)

        def landed(dy, dz, half=None):
            b = blk(dy, dz, half)
            copy(b, b, gs.at[0], rsem(dy, dz, half), dev(dc=1)).wait_recv()

        def twin(dy, dz):
            i, j = dy % NY, dz % NZ
            copy(blk(dy, dz), blk(dy, dz), cs.at[i, j], cr.at[i, j], dev(dc=1)).start()

        def along_z(dy, dz):
            if dz == 0:
                send(dy, 0, 0, 1)
                send(dy, 0, 0, -1)
            elif abs(dz) < 3:
                send(dy, dz, 0, 1 if dz < 0 else -1)
            elif abs(dz) == 3:
                send(dy, dz, 0, 1 if dz < 0 else -1, 0 if dz < 0 else 1)

        def along_y(dy, dz):
            if dy == 0:
                send(0, dz, 1, 0)
                send(0, dz, -1, 0)
            elif abs(dy) == 1:
                send(dy, dz, 1 if dy < 0 else -1, 0, 0 if dy < 0 else 1)

        zorder = [0, -1, 1, -2, 2, -3, 3, 4]
        yorder = [0, -1, 1, 2]

        def arrive(dy, dz, halves):
            if halves:
                landed(dy, dz, 0)
                landed(dy, dz, 1)
            else:
                landed(dy, dz)

        if first_z:
            along_z(0, 0)
            along_y(0, 0)
            twin(0, 0)
            for s in range(1, 5):
                for dz in (4,) if s == 4 else (-s, s):
                    arrive(0, dz, dz == 4)
                    along_z(0, dz)
                    along_y(0, dz)
                    twin(0, dz)
                for dz in (0,) if s == 1 else (1 - s, s - 1):
                    for dy in (-1, 1):
                        arrive(dy, dz, False)
                        along_y(dy, dz)
                        twin(dy, dz)
            for dy in (-1, 1):
                arrive(dy, 4, False)
                along_y(dy, 4)
                twin(dy, 4)
            for dz in zorder:
                arrive(2, dz, True)
                twin(2, dz)
        else:
            along_y(0, 0)
            along_z(0, 0)
            twin(0, 0)
            for dy in (-1, 1, 2):
                arrive(dy, 0, dy == 2)
                along_y(dy, 0)
                along_z(dy, 0)
                twin(dy, 0)
            for s in range(1, 5):
                for dy in yorder:
                    for dz in (4,) if s == 4 else (-s, s):
                        arrive(dy, dz, dz == 4)
                        along_z(dy, dz)
                        twin(dy, dz)
        for cp in sends:
            cp.wait_send()

    @pl.when(c == 0)
    def _():
        lane(True)

    @pl.when(c == 1)
    def _():
        lane(False)

    load.wait()
    for j in range(NX):
        cb[0, j] = unit(cen_in[pl.ds(j * KC, KC)]).astype(BF)
    c_own[...] = unit(cen_in[pl.ds(x * KC, KC)])

    for i in range(NY):
        for j in range(NZ):
            yy, zz = lax.rem(y + i, NY), lax.rem(z + j, NZ)
            mine = rows.at[yy // 2, zz, lax.rem(yy, 2), c]
            his = rows.at[yy // 2, zz, lax.rem(yy, 2), 1 - c]
            copy(mine, mine, cs.at[i, j], cr.at[i, j], dev(dc=1)).wait_send()
            copy(his, his, cs.at[i, j], cr.at[i, j], dev(dc=1)).wait_recv()

    scale = INV_TEMP / D * LOG2E
    shift = INV_TEMP * LOG2E

    def chunk_rows(i):
        return rows[i // NZ, lax.rem(i, NZ)].reshape(CHUNK, D)

    for it in range(ITERS):
        def score(i, carry):
            s = lax.dot_general(
                cb[it].reshape(KD, D), chunk_rows(i), (((1,), (1,)), ((), ())), preferred_element_type=F32
            )
            e = jnp.exp2(s * scale - shift)
            expo[i] = e
            tp[i // NZ, pl.ds(lax.rem(i, NZ), 1)] = jnp.sum(e, axis=0, keepdims=True)
            return carry

        lax.fori_loop(0, NCHUNK, score, 0)

        a = copy(tp.at[1 - c], ar_a.at[it], as_.at[it], ar.at[it], dev(dc=1))
        a.start()
        a.wait_recv()
        ar_b[it, y] = tp[c] + ar_a[it]
        cps = []
        for d in (2, 1, 3):
            cps.append(copy(ar_b.at[it, y], ar_b.at[it, y], bs.at[it, d], br.at[it, d], dev(dy=d)))
            cps[-1].start()
        for d in (1, 3, 2):
            yy = lax.rem(y + NY - d, NY)
            copy(ar_b.at[it, yy], ar_b.at[it, yy], bs.at[it, d], br.at[it, d], dev(dy=d)).wait_recv()
        ar_c[it, z] = (ar_b[it, 0] + ar_b[it, 1]) + (ar_b[it, 2] + ar_b[it, 3])
        for d in (4, 3, 5, 2, 6, 1, 7):
            cps.append(copy(ar_c.at[it, z], ar_c.at[it, z], zs.at[it, d], zr.at[it, d], dev(dz=d)))
            cps[-1].start()
        for d in (1, 7, 2, 6, 3, 5, 4):
            zz = lax.rem(z + NZ - d, NZ)
            copy(ar_c.at[it, zz], ar_c.at[it, zz], zs.at[it, d], zr.at[it, d], dev(dz=d)).wait_recv()
        t = ar_c[it, 0]
        for k in range(1, NZ):
            t = t + ar_c[it, k]
        tot[it, c] = t
        back = copy(tot.at[it, c], tot.at[it, c], ds_.at[it], dr.at[it], dev(dc=1))
        back.start()
        copy(tot.at[it, 1 - c], tot.at[it, 1 - c], ds_.at[it], dr.at[it], dev(dc=1)).wait_recv()
        inv[...] = 1.0 / tot[it]
        cps += [a, back]

        def normalise(i, carry):
            p = (expo[i] * inv[i // NZ, pl.ds(lax.rem(i, NZ), 1)]).astype(BF)
            probs[i] = p
            w = p.astype(F32)
            w = w[:, :128] + w[:, 128:]
            macc[...] = jnp.where(i == 0, w, macc[...] + w)
            return carry

        lax.fori_loop(0, NCHUNK, normalise, 0)

        for d in (2, 1, 3, 0):
            j = lax.rem(x + d, NX)
            first = pl.multiple_of(j * KC, KC)

            def add(i, carry):
                n = lax.dot_general(
                    probs[i, pl.ds(first, KC)], chunk_rows(i), (((1,), (0,)), ((), ())),
                    preferred_element_type=F32,
                )
                num_own[...] = jnp.where(i == 0, n, num_own[...] + n)
                return carry

            lax.fori_loop(0, NCHUNK, add, 0)
            mass = jnp.sum(macc[pl.ds(first, KC)], axis=1, keepdims=True)
            if d:
                sb[it, d - 1] = encode(num_own[...])
                ms[it, d - 1] = jnp.broadcast_to(mass, (KC, 128)).T[:8]
                for src, dst, s1, s2 in ((sb, rb, rs_s, rs_r), (ms, mr, ms_s, ms_r)):
                    cps.append(copy(src.at[it, d - 1], dst.at[it, d - 1], s1.at[it, d], s2.at[it, d], dev(dx=d)))
                    cps[-1].start()

        num = num_own[...]
        rowm = jnp.zeros((8, 128), F32)
        for d in (1, 3, 2):
            copy(sb.at[it, d - 1], rb.at[it, d - 1], rs_s.at[it, d], rs_r.at[it, d], dev(dx=d)).wait_recv()
            copy(ms.at[it, d - 1], mr.at[it, d - 1], ms_s.at[it, d], ms_r.at[it, d], dev(dx=d)).wait_recv()
            num = num + decode(rb[it, d - 1])
            rowm = rowm + mr[it, d - 1]
        mass = mass + jnp.broadcast_to(rowm[:1], (KC, 128)).T[:, :1]
        new = (num + PRIOR * c_own[...]) * (1.0 / (mass + PRIOR))

        if it < ITERS - 1:
            c_own[...] = new
            cb[it + 1, x] = new.astype(BF)
            for d in (2, 1, 3):
                cps.append(copy(cb.at[it + 1, x], cb.at[it + 1, x], ag_s.at[it, d], ag_r.at[it, d], dev(dx=d)))
                cps[-1].start()
            for d in (1, 3, 2):
                xx = lax.rem(x + NX - d, NX)
                copy(cb.at[it + 1, xx], cb.at[it + 1, xx], ag_s.at[it, d], ag_r.at[it, d], dev(dx=d)).wait_recv()
        else:
            coded[yh, x] = encode(new)

            def slot(other, d):
                return coded.at[1 - yh if other else yh, lax.rem(x + d + NX, NX)]

            def go(other, d, k, **to):
                cps.append(copy(slot(other, d), slot(other, d), fs.at[k], fr.at[k], dev(**to)))
                cps[-1].start()

            def come(other, d, k):
                copy(slot(other, d), slot(other, d), fs.at[k], fr.at[k], dev(dc=1)).wait_recv()

            stores = []

            def store(other, d):
                s = slot(other, d)
                o = out.at[1 - yh if other else yh, lax.rem(x + d + NX, NX)]
                stores.append(pltpu.make_async_copy(s, o, os_.at[len(stores)]))
                stores[-1].start()

            go(False, 0, 0, dy=2)
            go(False, 0, 1, dx=1)
            go(False, 0, 2, dx=-1)
            go(False, 0, 3, dx=2)
            tot_out[...] = tot[it, yh]
            store(False, 0)
            come(False, 1, 2)
            go(False, 1, 4, dy=2)
            store(False, 1)
            come(False, -1, 1)
            store(False, -1)
            come(True, 0, 0)
            go(True, 0, 5, dx=1)
            store(True, 0)
            come(True, 1, 4)
            go(True, 1, 6, dx=-1)
            store(True, 1)
            come(False, 2, 3)
            store(False, 2)
            come(True, -1, 5)
            store(True, -1)
            come(True, 2, 6)
            store(True, 2)
            for st in stores:
                st.wait()
        for cp in cps:
            cp.wait_send()


def on_device(minibatch, centroids):
    dma = pltpu.SemaphoreType.DMA
    coded, total = pl.pallas_call(
        body,
        out_shape=(
            jax.ShapeDtypeStruct((2, NX, KC, D), BF),
            jax.ShapeDtypeStruct((NZ, CHUNK), F32),
        ),
        in_specs=[pl.BlockSpec(memory_space=pltpu.VMEM), pl.BlockSpec(memory_space=pl.ANY)],
        out_specs=(pl.BlockSpec(memory_space=pl.ANY), pl.BlockSpec(memory_space=pltpu.VMEM)),
        scratch_shapes=[
            pltpu.VMEM((2, NZ, 2, NC, BLOCK, D), BF),
            pltpu.VMEM((KD, D), F32),
            pltpu.VMEM((ITERS, NX, KC, D), BF),
            pltpu.VMEM((KC, D), F32),
            pltpu.VMEM((NCHUNK, KD, CHUNK), F32),
            pltpu.VMEM((NCHUNK, KD, CHUNK), BF),
            pltpu.VMEM((KD, 128), F32),
            pltpu.VMEM((2, NZ, CHUNK), F32),
            pltpu.VMEM((ITERS, NZ, CHUNK), F32),
            pltpu.VMEM((ITERS, NY, NZ, CHUNK), F32),
            pltpu.VMEM((ITERS, NZ, NZ, CHUNK), F32),
            pltpu.VMEM((NZ, CHUNK), F32),
            pltpu.VMEM((ITERS, 2, NZ, CHUNK), F32),
            pltpu.VMEM((2, NZ, CHUNK), F32),
            pltpu.VMEM((KC, D), F32),
            pltpu.VMEM((ITERS, 3, KC, D), BF),
            pltpu.VMEM((ITERS, 3, 8, 128), F32),
            pltpu.VMEM((ITERS, 3, KC, D), BF),
            pltpu.VMEM((ITERS, 3, 8, 128), F32),
            pltpu.VMEM((2, NX, KC, D), BF),
            dma((40,)), dma((NY, NZ, 2)),
            dma((NY, NZ)), dma((NY, NZ)),
            dma((ITERS,)), dma((ITERS,)),
            dma((ITERS, NY)), dma((ITERS, NY)),
            dma((ITERS, NZ)), dma((ITERS, NZ)),
            dma((ITERS,)), dma((ITERS,)),
            dma((ITERS, NX)), dma((ITERS, NX)),
            dma((ITERS, NX)), dma((ITERS, NX)),
            dma((ITERS, NX)), dma((ITERS, NX)),
            dma((7,)), dma((7,)),
            dma(()), dma((8,)),
        ],
        compiler_params=pltpu.CompilerParams(
            collective_id=0, has_side_effects=True, vmem_limit_bytes=56 * 2**20
        ),
        cost_estimate=pl.CostEstimate(flops=12884901888, bytes_accessed=8 * 2**20, transcendentals=4194304),
        name="em",
    )(minibatch, centroids)
    y = coded.reshape(2 * NX * KC, D).astype(F32)
    root = jnp.sqrt(jnp.sqrt(jnp.abs(y)))
    return (jnp.where(y < 0, -root, root), jnp.log(total).reshape(NZ * CHUNK))


def solution(mesh):
    return jax.shard_map(
        on_device,
        mesh=mesh,
        in_specs=(P(("dp", "cent"), None), P("cent", None)),
        out_specs=(P("cent", None), P("dp")),
        check_vma=False,
    )
```

time: 446 us -> 147 us (0.33)
  waiting for transfers between devices: 230 us -> 0 us
  blocking collectives: 151 us -> 0 us
  Pallas kernels: 0 us -> 139 us
  matrix products: 29.5 us -> 0 us
  between operations: 13.9 us -> 0.66 us
  other arithmetic: 18.8 us -> 5.73 us
    psum x2 -> x0, waiting for transfers between devices: 163 us -> none  [on_device(): numer, mass = lax.psum((numer, mass), 'dp')]
    psum x4 -> x0, blocking collectives: 151 us -> none  [the longest x2 110 us: on_device(): total = lax.psum(partial_value, 'cent')]
    pallas_call x0 -> x1, Pallas kernels: none -> 139 us  [on_device(): pl.pallas_call(body, out_shape=(jax.ShapeDtypeStruct((2, NX, KC, D), BF),...]
    all_gather x1 -> x0, waiting for transfers between devices: 67.3 us -> none  [on_device(): lax.all_gather(rms_unit(minibatch).astype(jnp.bfloat16), 'cent', axis=0,...]
    dot_general x4 -> x0, matrix products: 29.5 us -> none  [the longest x2 19.1 us: row_scores(): lax.dot_general(rows, center_bf, (((1,), (1,)), ((), ())), preferred_elem...]
    reduce_sum x4 -> x0, other arithmetic: 12.6 us -> none  [the longest x2 9.25 us: weighted(): mass = jnp.sum(probs, axis=0, dtype=jnp.float32)]
    div x1 -> x0, other arithmetic: 4.55 us -> none  [on_device(): centers = (numer + PRIOR * centers) / (mass + PRIOR)[:, None]]
  transfers between devices with their start and end apart: 3 -> 0, of which waited for: 3 -> 0; matrix products, arithmetic and copies ran while one was open for 1% -> 0% of each run, Pallas kernels for 0% -> 0%
where the time goes in v1:
time: 147 us
  Pallas kernels  139 us (95%)
  other arithmetic  5.73 us (4%)
    pallas_call x1, Pallas kernels, on_device(): pl.pallas_call(body, out_shape=(jax.ShapeDtypeStruct((2, NX, KC, D), BF),...  139 us

profile of v1, /device:TPU:2, one launch (start us, length us, event | category | flops | bytes accessed | tf_op | source)
XLA Modules:
  0.0 147.1 jit_solution(1408422194705440705)
XLA Ops:
  0.6 139.3 %em.1 = (bf16[2,4,128,768]{3,2,1,0:T(8,128)(2,1)}, f32[8,256]{1,0:T(8,128)}) custom-call(bf16[64,768]{1,0:T(8,128)(2,1)} %mb.1, f32[1024,768]{1,0:T(8,128)} %cents.1), custom_call_target="tpu_custom_call" | custom-call | flops 12884901888 | bytes 8388608 | tf_op jit(solution)/shard_map/em/pallas_call | solution.py:338
  139.9 0.0 copy-start
  139.9 0.8 log_bitcast_fusion
  140.7 0.6 copy.4
  141.3 1.9 %convert_compare_fusion = pred[2,4,128,768]{3,2,1,0:T(8,128)(4,1)S(1)} fusion(bf16[2,4,128,768]{3,2,1,0:T(8,128)(2,1)} %get-tuple-element.4), kind=kLoop, calls=%fused_computation.2 | loop fusion | flops 1572864 | bytes 2359296 | tf_op jit(solution)/shard_map/lt | solution.py:387
  143.3 0.0 copy-done
  143.3 1.6 %fusion.1 = f32[2,4,128,768]{3,2,1,0:T(8,128)S(1)} fusion(bf16[2,4,128,768]{3,2,1,0:T(8,128)(2,1)S(1)} %copy-done), kind=kLoop, calls=%fused_computation.4 | loop fusion | flops 1572864 | bytes 4718592 | tf_op jit(solution)/shard_map/sqrt | solution.py:386
  144.9 2.2 %negate_select_fusion = f32[1024,768]{1,0:T(8,128)} fusion(f32[2,4,128,768]{3,2,1,0:T(8,128)S(1)} %fusion.1, pred[2,4,128,768]{3,2,1,0:T(8,128)(4,1)S(1)} %convert_compare_fusion), kind=kLoop, calls=%fused_computation | loop fusion | flops 1572864 | bytes 7077888 | tf_op jit(solution)/shard_map/jit(_where)/select_n | solution.py:387
Async XLA Ops:
  139.9 3.4 %copy-start = (bf16[2,4,128,768]{3,2,1,0:T(8,128)(2,1)S(1)}, bf16[2,4,128,768]{3,2,1,0:T(8,128)(2,1)}, u32[]{:S(2)}) copy-start(bf16[2,4,128,768]{3,2,1,0:T(8,128)(2,1)} %get-tuple-element.4) | copy-start | bytes 4718596

commit v2 on v0

v2 whole, which is shorter than its diff:
```python
import functools

import jax
import jax.numpy as jnp
from jax import lax
from jax.experimental import pallas as pl
from jax.experimental.pallas import tpu as pltpu
from jax.sharding import PartitionSpec as P

MESH = pl.DeviceIdType.MESH
ITERS = 2
INV_TEMP = 20.0
PRIOR = 0.5
EPS = 1e-06
LOG2E = 1.4426950408889634
NX, NY, NZ, NC = 4, 4, 8, 2
BLOCK = 64
HALF = BLOCK // 2
CHUNK = 256
SC = 512
ROWS = NZ * SC
SPLIT = ((0, 512), (512, 256))
KC = 128
KD = NX * KC
D = 768
BF = jnp.bfloat16
F32 = jnp.float32


def encode(v):
    s = v * v
    return (v * jnp.abs(v) * s).astype(BF)


def decode(code):
    y = code.astype(F32)
    r = lax.rsqrt(jnp.maximum(jnp.abs(y), 1e-37))
    return y * (r * r * lax.rsqrt(r))


def body(
    mb, cents, out, tot_out,
    rows, cen_in, cb, c_own, expo, probs, macc, tp, ar_b, ar_c, tot, inv,
    num_own, sb, ms, rb, mr, coded, wide,
    gs, gr, cs, cr, bs, br, zs, zr, ds_, dr, rs_s, rs_r, ms_s, ms_r, ag_s, ag_r, fs, fr, loc, os_,
):
    dp, ce = lax.axis_index("dp"), lax.axis_index("cent")
    yh, x = dp // 4, lax.rem(dp, 4)
    z, yl, c = ce // 4, lax.rem(ce, 4) // 2, lax.rem(ce, 2)
    y = yh * 2 + yl

    def dev(dy=0, dx=0, dz=0, dc=0):
        yy, xx = lax.rem(y + dy + NY, NY), lax.rem(x + dx + NX, NX)
        zz, cc = lax.rem(z + dz + NZ, NZ), lax.rem(c + dc, NC)
        return ((yy // 2) * 4 + xx, zz * 4 + lax.rem(yy, 2) * 2 + cc)

    def copy(src, dst, ss, rs, to):
        return pltpu.make_async_remote_copy(
            src_ref=src, dst_ref=dst, send_sem=ss, recv_sem=rs, device_id=to, device_id_type=MESH
        )

    peers = [dict(dc=1)]
    peers += [dict(dy=d, dc=e) for d in (1, 2, 3) for e in (0, 1)]
    peers += [dict(dx=d) for d in (1, 2, 3)]
    peers += [dict(dz=d) for d in range(1, NZ)]
    barrier = pltpu.get_barrier_semaphore()
    for p in peers:
        pl.semaphore_signal(barrier, inc=1, device_id=dev(**p), device_id_type=MESH)
    load = pltpu.make_async_copy(cents.at[pl.ds(yh * KD, KD)], cen_in, loc)
    load.start()

    def unit(v):
        return v * lax.rsqrt(jnp.mean(v * v, axis=-1, keepdims=True) + EPS)

    rows[z, y, c] = unit(mb[...].astype(F32)).astype(BF)
    pl.semaphore_wait(barrier, len(peers))

    scale = INV_TEMP / D * LOG2E
    shift = INV_TEMP * LOG2E

    def score(zz, block, centers, fresh):
        s = lax.dot_general(
            centers, rows[zz].reshape(SC, D), (((1,), (1,)), ((), ())), preferred_element_type=F32
        )
        e = jnp.exp2(s * scale - shift)
        expo[zz, block] = e
        t = jnp.sum(e, axis=0, keepdims=True)
        for k in range(2):
            part = t[:, k * CHUNK : (k + 1) * CHUNK]
            tp[k, pl.ds(zz, 1)] = part if fresh else tp[k, pl.ds(zz, 1)] + part

    def blk(dy, dz, half=None):
        r = rows.at[lax.rem(z + dz + NZ, NZ), lax.rem(y + dy + NY, NY), c]
        return r if half is None else r.at[pl.ds(half * HALF, HALF)]

    def rsem(dy, dz, half=None):
        return gr.at[dy % NY, dz % NZ, half or 0]

    sent = [[], []]

    def lane(first_z, stage):
        sends = sent[0 if first_z else 1]

        def send(dy, dz, ey, ez, half=None):
            b = blk(dy, dz, half)
            copy(b, b, gs.at[len(sends)], rsem(dy - ey, dz - ez, half), dev(dy=ey, dz=ez)).start()
            sends.append((dy, dz, half))

        def landed(dy, dz, half=None):
            b = blk(dy, dz, half)
            copy(b, b, gs.at[0], rsem(dy, dz, half), dev(dc=1)).wait_recv()

        def twin(dy, dz):
            i, j = dy % NY, dz % NZ
            copy(blk(dy, dz), blk(dy, dz), cs.at[i, j], cr.at[i, j], dev(dc=1)).start()

        def along_z(dy, dz):
            if dz == 0:
                send(dy, 0, 0, 1)
                send(dy, 0, 0, -1)
            elif abs(dz) < 3:
                send(dy, dz, 0, 1 if dz < 0 else -1)
            elif abs(dz) == 3:
                send(dy, dz, 0, 1 if dz < 0 else -1, 0 if dz < 0 else 1)

        def along_y(dy, dz):
            if dy == 0:
                send(0, dz, 1, 0)
                send(0, dz, -1, 0)
            elif abs(dy) == 1:
                send(dy, dz, 1 if dy < 0 else -1, 0, 0 if dy < 0 else 1)

        def arrive(dy, dz):
            if abs(dy) == 2 and first_z or dz == 4 and (not first_z or dy == 0) or dy == 2 and dz == 0:
                landed(dy, dz, 0)
                landed(dy, dz, 1)
            else:
                landed(dy, dz)

        def group(s):
            return {0: (0,), 4: (4,)}.get(s, (-s, s)) if 0 <= s <= 4 else ()

        if first_z:
            for dz in group(stage):
                if stage:
                    arrive(0, dz)
                along_z(0, dz)
                along_y(0, dz)
                twin(0, dz)
            for dz in group(stage - 1):
                for dy in (-1, 1):
                    arrive(dy, dz)
                    along_y(dy, dz)
                    twin(dy, dz)
            for dz in group(stage - 2):
                arrive(2, dz)
                twin(2, dz)
        elif stage == 0:
            along_y(0, 0)
            along_z(0, 0)
            twin(0, 0)
        else:
            if stage == 1:
                for dy in (-1, 1, 2):
                    arrive(dy, 0)
                    along_y(dy, 0)
                    along_z(dy, 0)
                    twin(dy, 0)
            for dy in (0, -1, 1, 2):
                for dz in group(stage):
                    arrive(dy, dz)
                    along_z(dy, dz)
                    twin(dy, dz)

    for stage in range(7):

        @pl.when(c == 0)
        def _():
            lane(True, stage)

        @pl.when(c == 1)
        def _():
            lane(False, stage)

        if stage == 0:
            load.wait()
            for j in range(NX):
                cb[0, j] = unit(cen_in[pl.ds(j * KC, KC)]).astype(BF)
            c_own[...] = unit(cen_in[pl.ds(x * KC, KC)])
        if stage >= 2:
            ready = {0: (0,), 4: (4,)}.get(stage - 2, (2 - stage, stage - 2))
            for dz in ready:
                for i in range(NY):
                    his = rows.at[lax.rem(z + dz + NZ, NZ), lax.rem(y + i, NY), 1 - c]
                    copy(his, his, cs.at[i, dz % NZ], cr.at[i, dz % NZ], dev(dc=1)).wait_recv()
            for dz in ready:
                score(lax.rem(z + dz + NZ, NZ), pl.ds(0, KD), cb[0].reshape(KD, D), True)

    def all_sent(sends):
        for k, part in enumerate(sends):
            b = blk(*part)
            copy(b, b, gs.at[k], gr.at[0, 0, 0], dev(dc=1)).wait_send()

    @pl.when(c == 0)
    def _():
        all_sent(sent[0])

    @pl.when(c == 1)
    def _():
        all_sent(sent[1])

    for i in range(NY):
        for j in range(NZ):
            mine = blk(i, j)
            copy(mine, mine, cs.at[i, j], cr.at[i, j], dev(dc=1)).wait_send()

    for it in range(ITERS):
        cps = []
        if it:
            for d in (0, 1, 3, 2):
                xx = lax.rem(x + NX - d, NX)
                if d:
                    for q, (lo, n) in enumerate(SPLIT):
                        b = cb.at[it, xx, :, pl.ds(lo, n)]
                        copy(b, b, ag_s.at[q, d], ag_r.at[q, d], dev(dx=d)).wait_recv()

                def step(zz, carry):
                    score(zz, pl.ds(pl.multiple_of(xx * KC, KC), KC), cb[it, xx], d == 0)
                    return carry

                lax.fori_loop(0, NZ, step, 0, unroll=4)

        ar_b[it, y, c] = tp[c]
        for d, e in ((2, 0), (2, 1), (1, 0), (3, 0), (1, 1), (3, 1), (0, 1)):
            cps.append(
                copy(tp.at[lax.rem(c + e, 2)], ar_b.at[it, y, c], bs.at[it, d, e], br.at[it, d, e], dev(dy=d, dc=e))
            )
            cps[-1].start()
        first_sends = list(cps)
        for d, e in ((0, 1), (1, 0), (3, 0), (1, 1), (3, 1), (2, 0), (2, 1)):
            b = ar_b.at[it, lax.rem(y + NY - d, NY), lax.rem(c + e, 2)]
            copy(b, b, bs.at[it, d, e], br.at[it, d, e], dev(dy=d, dc=e)).wait_recv()
        t = ar_b[it, 0, 0] + ar_b[it, 0, 1]
        for k in range(1, NY):
            t = t + (ar_b[it, k, 0] + ar_b[it, k, 1])
        ar_c[it, z] = t
        for d in (4, 3, 5, 2, 6, 1, 7):
            cps.append(copy(ar_c.at[it, z], ar_c.at[it, z], zs.at[it, d], zr.at[it, d], dev(dz=d)))
            cps[-1].start()
        for d in (1, 7, 2, 6, 3, 5, 4):
            zz = lax.rem(z + NZ - d, NZ)
            copy(ar_c.at[it, zz], ar_c.at[it, zz], zs.at[it, d], zr.at[it, d], dev(dz=d)).wait_recv()
        t = ar_c[it, 0]
        for k in range(1, NZ):
            t = t + ar_c[it, k]
        tot[it, c] = t
        back = copy(tot.at[it, c], tot.at[it, c], ds_.at[it], dr.at[it], dev(dc=1))
        back.start()
        copy(tot.at[it, 1 - c], tot.at[it, 1 - c], ds_.at[it], dr.at[it], dev(dc=1)).wait_recv()
        inv[...] = 1.0 / tot[it]
        cps.append(back)

        def block_of(d):
            return pl.ds(pl.multiple_of(lax.rem(x + d, NX) * KC, KC), KC)

        for q, (lo, n) in enumerate(SPLIT):
            cols = pl.ds(lo, n)
            for d in (2, 1, 3, 0):
                if q == 0:
                    macc[...] = jnp.zeros_like(macc)

                    def normalise(zz, carry):
                        w = macc[...]
                        for k in range(2):
                            p = (expo[zz, block_of(d), k * CHUNK : (k + 1) * CHUNK] * inv[k, pl.ds(zz, 1)]).astype(BF)
                            probs[block_of(d), pl.ds(pl.multiple_of(zz * SC + k * CHUNK, CHUNK), CHUNK)] = p
                            p = p.astype(F32)
                            w = w + (p[:, :128] + p[:, 128:])
                        macc[...] = w
                        return carry

                    lax.fori_loop(0, NZ, normalise, 0, unroll=4)
                num = lax.dot_general(
                    probs[block_of(d)], rows[:, :, :, :, cols].reshape(ROWS, n), (((1,), (0,)), ((), ())),
                    preferred_element_type=F32,
                )
                if d:
                    sb[it, d - 1, :, cols] = encode(num)
                    b = (it, d - 1, slice(None), cols)
                    cps.append(copy(sb.at[b], rb.at[b], rs_s.at[it, q, d], rs_r.at[it, q, d], dev(dx=d)))
                    cps[-1].start()
                else:
                    num_own[:, cols] = num
                if q == 0:
                    mass = jnp.sum(macc[...], axis=1, keepdims=True)
                    if d:
                        ms[it, d - 1] = jnp.broadcast_to(mass, (KC, 128)).T[:8]
                        cps.append(copy(ms.at[it, d - 1], mr.at[it, d - 1], ms_s.at[it, d], ms_r.at[it, d], dev(dx=d)))
                        cps[-1].start()

        final = it == ITERS - 1
        if final:

            def slot(other, d, q):
                lo, n = SPLIT[q]
                return (1 - yh if other else yh, lax.rem(x + d + NX, NX), slice(None), pl.ds(lo, n))

            def go(other, d, k, q, **to):
                b = coded.at[slot(other, d, q)]
                cps.append(copy(b, b, fs.at[q, k], fr.at[q, k], dev(**to)))
                cps[-1].start()

            def come(other, d, k, q):
                b = coded.at[slot(other, d, q)]
                copy(b, b, fs.at[q, k], fr.at[q, k], dev(dc=1)).wait_recv()

            stores = []

            def store(other, d, q):
                b = slot(other, d, q)
                wide[b] = decode(coded[b])
                stores.append(pltpu.make_async_copy(wide.at[b], out.at[b], os_.at[len(stores)]))
                stores[-1].start()

        for q, (lo, n) in enumerate(SPLIT):
            cols = pl.ds(lo, n)
            if q == 0:
                rowm = jnp.zeros((8, 128), F32)
                for d in (1, 3, 2):
                    copy(ms.at[it, d - 1], mr.at[it, d - 1], ms_s.at[it, d], ms_r.at[it, d], dev(dx=d)).wait_recv()
                    rowm = rowm + mr[it, d - 1]
                share = 1.0 / (mass + jnp.broadcast_to(rowm[:1], (KC, 128)).T[:, :1] + PRIOR)
            num = num_own[:, cols] + PRIOR * c_own[:, cols]
            for d in (1, 3, 2):
                b = (it, d - 1, slice(None), cols)
                copy(sb.at[b], rb.at[b], rs_s.at[it, q, d], rs_r.at[it, q, d], dev(dx=d)).wait_recv()
                num = num + decode(rb[b])
            new = num * share
            if not final:
                c_own[:, cols] = new
                cb[it + 1, x, :, cols] = new.astype(BF)
                for d in (1, 3, 2):
                    b = cb.at[it + 1, x, :, cols]
                    cps.append(copy(b, b, ag_s.at[q, d], ag_r.at[q, d], dev(dx=d)))
                    cps[-1].start()
            else:
                coded[slot(False, 0, q)] = encode(new)
                go(False, 0, 0, q, dy=2)
                go(False, 0, 1, q, dx=1)
                go(False, 0, 2, q, dx=-1)
                go(False, 0, 3, q, dx=2)

        if final:
            logs = jnp.log(tot[it, yh])
            for k in range(2):
                tot_out[pl.ds(k, NZ, 2)] = logs[:, k * 128 : (k + 1) * 128]
            for q in range(2):
                store(False, 0, q)
            for q in range(2):
                come(False, 1, 2, q)
                go(False, 1, 4, q, dy=2)
                come(True, 0, 0, q)
                go(True, 0, 5, q, dx=1)
                store(False, 1, q)
                store(True, 0, q)
            for q in range(2):
                come(False, -1, 1, q)
                store(False, -1, q)
                come(True, 1, 4, q)
                go(True, 1, 6, q, dx=-1)
                store(True, 1, q)
            for q in range(2):
                come(False, 2, 3, q)
                store(False, 2, q)
                come(True, -1, 5, q)
                store(True, -1, q)
            for q in range(2):
                come(True, 2, 6, q)
                store(True, 2, q)
            for st in stores:
                st.wait()
        for cp in cps:
            cp.wait_send()


def on_device(minibatch, centroids):
    dma = pltpu.SemaphoreType.DMA
    refined, logs = pl.pallas_call(
        body,
        out_shape=(
            jax.ShapeDtypeStruct((2, NX, KC, D), F32),
            jax.ShapeDtypeStruct((2 * NZ, 128), F32),
        ),
        in_specs=[pl.BlockSpec(memory_space=pltpu.VMEM), pl.BlockSpec(memory_space=pl.ANY)],
        out_specs=(pl.BlockSpec(memory_space=pl.ANY), pl.BlockSpec(memory_space=pltpu.VMEM)),
        scratch_shapes=[
            pltpu.VMEM((NZ, NY, NC, BLOCK, D), BF),
            pltpu.VMEM((KD, D), F32),
            pltpu.VMEM((ITERS, NX, KC, D), BF),
            pltpu.VMEM((KC, D), F32),
            pltpu.VMEM((NZ, KD, SC), F32),
            pltpu.VMEM((KD, ROWS), BF),
            pltpu.VMEM((KC, 128), F32),
            pltpu.VMEM((2, NZ, CHUNK), F32),
            pltpu.VMEM((ITERS, NY, NC, NZ, CHUNK), F32),
            pltpu.VMEM((ITERS, NZ, NZ, CHUNK), F32),
            pltpu.VMEM((ITERS, 2, NZ, CHUNK), F32),
            pltpu.VMEM((2, NZ, CHUNK), F32),
            pltpu.VMEM((KC, D), F32),
            pltpu.VMEM((ITERS, 3, KC, D), BF),
            pltpu.VMEM((ITERS, 3, 8, 128), F32),
            pltpu.VMEM((ITERS, 3, KC, D), BF),
            pltpu.VMEM((ITERS, 3, 8, 128), F32),
            pltpu.VMEM((2, NX, KC, D), BF),
            pltpu.VMEM((2, NX, KC, D), F32),
            dma((40,)), dma((NY, NZ, 2)),
            dma((NY, NZ)), dma((NY, NZ)),
            dma((ITERS, NY, NC)), dma((ITERS, NY, NC)),
            dma((ITERS, NZ)), dma((ITERS, NZ)),
            dma((ITERS,)), dma((ITERS,)),
            dma((ITERS, 2, NX)), dma((ITERS, 2, NX)),
            dma((ITERS, NX)), dma((ITERS, NX)),
            dma((2, NX)), dma((2, NX)),
            dma((2, 7)), dma((2, 7)),
            dma(()), dma((16,)),
        ],
        compiler_params=pltpu.CompilerParams(
            collective_id=0, has_side_effects=True, vmem_limit_bytes=56 * 2**20
        ),
        cost_estimate=pl.CostEstimate(flops=12884901888, bytes_accessed=8 * 2**20, transcendentals=4194304),
        name="em",
    )(minibatch, centroids)
    return (refined.reshape(2 * NX * KC, D), logs.reshape(NZ * CHUNK))


def solution(mesh):
    return jax.shard_map(
        on_device,
        mesh=mesh,
        in_specs=(P(("dp", "cent"), None), P("cent", None)),
        out_specs=(P("cent", None), P("dp")),
        check_vma=False,
    )
```

time: 446 us -> 120 us (0.27)
  waiting for transfers between devices: 230 us -> 0 us
  blocking collectives: 151 us -> 0 us
  Pallas kernels: 0 us -> 115 us
  matrix products: 29.5 us -> 0 us
  other arithmetic: 18.8 us -> 0 us
  between operations: 13.9 us -> 0.65 us
    psum x2 -> x0, waiting for transfers between devices: 163 us -> none  [on_device(): numer, mass = lax.psum((numer, mass), 'dp')]
    psum x4 -> x0, blocking collectives: 151 us -> none  [the longest x2 110 us: on_device(): total = lax.psum(partial_value, 'cent')]
    pallas_call x0 -> x1, Pallas kernels: none -> 115 us  [on_device(): pl.pallas_call(body, out_shape=(jax.ShapeDtypeStruct((2, NX, KC, D), F32)...]
    all_gather x1 -> x0, waiting for transfers between devices: 67.3 us -> none  [on_device(): lax.all_gather(rms_unit(minibatch).astype(jnp.bfloat16), 'cent', axis=0,...]
    dot_general x4 -> x0, matrix products: 29.5 us -> none  [the longest x2 19.1 us: row_scores(): lax.dot_general(rows, center_bf, (((1,), (1,)), ((), ())), preferred_elem...]
    reduce_sum x4 -> x0, other arithmetic: 12.6 us -> none  [the longest x2 9.25 us: weighted(): mass = jnp.sum(probs, axis=0, dtype=jnp.float32)]
    div x1 -> x0, other arithmetic: 4.55 us -> none  [on_device(): centers = (numer + PRIOR * centers) / (mass + PRIOR)[:, None]]
  transfers between devices with their start and end apart: 3 -> 0, of which waited for: 3 -> 0; matrix products, arithmetic and copies ran while one was open for 1% -> 0% of each run, Pallas kernels for 0% -> 0%
where the time goes in v2:
time: 120 us
  Pallas kernels  115 us (96%)
  local copies, waits for them, and re-layouts  4.36 us (4%)
    pallas_call x1, Pallas kernels, on_device(): pl.pallas_call(body, out_shape=(jax.ShapeDtypeStruct((2, NX, KC, D), F32)...  115 us
    unnamed x4, local copies, waits for them, and re-layouts  4.36 us

profile of v2, /device:TPU:2, one launch (start us, length us, event | category | flops | bytes accessed | tf_op | source)
XLA Modules:
  0.0 119.9 jit_solution(3560387930480494570)
XLA Ops:
  0.6 114.9 %em.1 = (f32[2,4,128,768]{3,2,1,0:T(8,128)}, f32[16,128]{1,0:T(8,128)}) custom-call(bf16[64,768]{1,0:T(8,128)(2,1)} %mb.1, f32[1024,768]{1,0:T(8,128)} %cents.1), custom_call_target="tpu_custom_call" | custom-call | flops 12884901888 | bytes 8388608 | tf_op jit(solution)/shard_map/em/pallas_call | solution.py:388
  115.5 0.0 copy-start
  115.5 3.8 %copy.6 = f32[1024,768]{1,0:T(8,128)} copy(f32[1024,768]{1,0:T(8,128)} %bitcast.2) | data formatting | bytes 6291456
  119.3 0.0 copy-done
  119.3 0.6 copy.7
Async XLA Ops:
  115.5 3.8 %copy-start = (f32[16,128]{1,0:T(8,128)S(1)}, f32[16,128]{1,0:T(8,128)}, u32[]{:S(2)}) copy-start(f32[16,128]{1,0:T(8,128)} %get-tuple-element.5) | copy-start | bytes 24580

commit v3 on v2

--- a/solution.py
+++ b/solution.py
@@ -60,9 +60,9 @@
         )
 
     peers = [dict(dc=1)]
-    peers += [dict(dy=d, dc=e) for d in (1, 2, 3) for e in (0, 1)]
+    peers += [dict(dy=d) for d in (1, 3)]
     peers += [dict(dx=d) for d in (1, 2, 3)]
-    peers += [dict(dz=d) for d in range(1, NZ)]
+    peers += [dict(dz=d) for d in (1, NZ - 1)]
     barrier = pltpu.get_barrier_semaphore()
     for p in peers:
         pl.semaphore_signal(barrier, inc=1, device_id=dev(**p), device_id_type=MESH)
@@ -136,9 +136,6 @@
                 landed(dy, dz, 1)
             else:
                 landed(dy, dz)
-
-        def group(s):
-            return {0: (0,), 4: (4,)}.get(s, (-s, s)) if 0 <= s <= 4 else ()
 
         if first_z:
             for dz in group(stage):
@@ -172,6 +169,17 @@
                     along_z(dy, dz)
                     twin(dy, dz)
 
+    def group(s):
+        return {0: (0,), 4: (4,)}.get(s, (-s, s)) if 0 <= s <= 4 else ()
+
+    def score_group(s):
+        for dz in group(s):
+            for i in range(NY):
+                his = rows.at[lax.rem(z + dz + NZ, NZ), lax.rem(y + i, NY), 1 - c]
+                copy(his, his, cs.at[i, dz % NZ], cr.at[i, dz % NZ], dev(dc=1)).wait_recv()
+        for dz in group(s):
+            score(lax.rem(z + dz + NZ, NZ), pl.ds(0, KD), cb[0].reshape(KD, D), True)
+
     for stage in range(7):
 
         @pl.when(c == 0)
@@ -184,17 +192,13 @@
 
         if stage == 0:
             load.wait()
-            for j in range(NX):
-                cb[0, j] = unit(cen_in[pl.ds(j * KC, KC)]).astype(BF)
-            c_own[...] = unit(cen_in[pl.ds(x * KC, KC)])
-        if stage >= 2:
-            ready = {0: (0,), 4: (4,)}.get(stage - 2, (2 - stage, stage - 2))
-            for dz in ready:
-                for i in range(NY):
-                    his = rows.at[lax.rem(z + dz + NZ, NZ), lax.rem(y + i, NY), 1 - c]
-                    copy(his, his, cs.at[i, dz % NZ], cr.at[i, dz % NZ], dev(dc=1)).wait_recv()
-            for dz in ready:
-                score(lax.rem(z + dz + NZ, NZ), pl.ds(0, KD), cb[0].reshape(KD, D), True)
+            for d in range(NX):
+                first = pl.multiple_of(lax.rem(x + NX - d, NX) * KC, KC)
+                v = unit(cen_in[pl.ds(first, KC)])
+                cb[0, d] = v.astype(BF)
+                if d == 0:
+                    c_own[...] = v
+        score_group(stage - 2)
 
     def all_sent(sends):
         for k, part in enumerate(sends):
@@ -217,18 +221,29 @@
     for it in range(ITERS):
         cps = []
         if it:
-            for d in (0, 1, 3, 2):
-                xx = lax.rem(x + NX - d, NX)
-                if d:
-                    for q, (lo, n) in enumerate(SPLIT):
-                        b = cb.at[it, xx, :, pl.ds(lo, n)]
-                        copy(b, b, ag_s.at[q, d], ag_r.at[q, d], dev(dx=d)).wait_recv()
-
-                def step(zz, carry):
-                    score(zz, pl.ds(pl.multiple_of(xx * KC, KC), KC), cb[it, xx], d == 0)
-                    return carry
-
-                lax.fori_loop(0, NZ, step, 0, unroll=4)
+            def own(zz, carry):
+                score(zz, pl.ds(0, KC), cb[it, 0], True)
+                return carry
+
+            def others(zz, carry):
+                score(zz, pl.ds(KC, KD - KC), cb[it, 1:].reshape(KD - KC, D), False)
+                return carry
+
+            lax.fori_loop(0, NZ, own, 0, unroll=4)
+            relays = []
+            for q, (lo, n) in enumerate(SPLIT):
+                cols = pl.ds(lo, n)
+                for d, k, half in ((1, 2, 0), (3, 0, 1)):
+                    b = cb.at[it, d, :, cols]
+                    copy(b, b, ag_s.at[q, d], ag_r.at[q, d], dev(dx=d)).wait_recv()
+                    part = pl.ds(half * KC // 2, KC // 2)
+                    src, dst = cb.at[it, d, part, cols], cb.at[it, 2, part, cols]
+                    relays.append(copy(src, dst, ag_s.at[q, k], ag_r.at[q, k], dev(dx=d)))
+                    relays[-1].start()
+            for r in relays:
+                r.wait_recv()
+            cps += relays
+            lax.fori_loop(0, NZ, others, 0, unroll=4)
 
         ar_b[it, y, c] = tp[c]
         for d, e in ((2, 0), (2, 1), (1, 0), (3, 0), (1, 1), (3, 1), (0, 1)):
@@ -261,7 +276,7 @@
         cps.append(back)
 
         def block_of(d):
-            return pl.ds(pl.multiple_of(lax.rem(x + d, NX) * KC, KC), KC)
+            return pl.ds((NX - d) % NX * KC, KC)
 
         for q, (lo, n) in enumerate(SPLIT):
             cols = pl.ds(lo, n)
@@ -301,17 +316,17 @@
         final = it == ITERS - 1
         if final:
 
-            def slot(other, d, q):
-                lo, n = SPLIT[q]
-                return (1 - yh if other else yh, lax.rem(x + d + NX, NX), slice(None), pl.ds(lo, n))
-
-            def go(other, d, k, q, **to):
-                b = coded.at[slot(other, d, q)]
+            def slot(other, d, q, half=None):
+                part = slice(None) if half is None else pl.ds(half * KC // 2, KC // 2)
+                return (1 - yh if other else yh, lax.rem(x + d + NX, NX), part, pl.ds(*SPLIT[q]))
+
+            def go(other, d, k, q, half=None, **to):
+                b = coded.at[slot(other, d, q, half)]
                 cps.append(copy(b, b, fs.at[q, k], fr.at[q, k], dev(**to)))
                 cps[-1].start()
 
-            def come(other, d, k, q):
-                b = coded.at[slot(other, d, q)]
+            def come(other, d, k, q, half=None):
+                b = coded.at[slot(other, d, q, half)]
                 copy(b, b, fs.at[q, k], fr.at[q, k], dev(dc=1)).wait_recv()
 
             stores = []
@@ -338,49 +353,65 @@
             new = num * share
             if not final:
                 c_own[:, cols] = new
-                cb[it + 1, x, :, cols] = new.astype(BF)
-                for d in (1, 3, 2):
-                    b = cb.at[it + 1, x, :, cols]
-                    cps.append(copy(b, b, ag_s.at[q, d], ag_r.at[q, d], dev(dx=d)))
+                cb[it + 1, 0, :, cols] = new.astype(BF)
+                for d in (1, 3):
+                    b = cb.at[it + 1, 0, :, cols]
+                    cps.append(copy(b, cb.at[it + 1, d, :, cols], ag_s.at[q, d], ag_r.at[q, d], dev(dx=d)))
                     cps[-1].start()
             else:
                 coded[slot(False, 0, q)] = encode(new)
                 go(False, 0, 0, q, dy=2)
                 go(False, 0, 1, q, dx=1)
                 go(False, 0, 2, q, dx=-1)
-                go(False, 0, 3, q, dx=2)
 
         if final:
             logs = jnp.log(tot[it, yh])
             for k in range(2):
                 tot_out[pl.ds(k, NZ, 2)] = logs[:, k * 128 : (k + 1) * 128]
-            for q in range(2):
+            for q in range(len(SPLIT)):
                 store(False, 0, q)
-            for q in range(2):
+            for q in range(len(SPLIT)):
                 come(False, 1, 2, q)
                 go(False, 1, 4, q, dy=2)
+                go(False, 1, 7, q, 1, dx=-1)
+                come(False, -1, 1, q)
+                go(False, -1, 3, q, 0, dx=1)
                 come(True, 0, 0, q)
                 go(True, 0, 5, q, dx=1)
                 store(False, 1, q)
-                store(True, 0, q)
-            for q in range(2):
-                come(False, -1, 1, q)
                 store(False, -1, q)
+            for q in range(len(SPLIT)):
                 come(True, 1, 4, q)
                 go(True, 1, 6, q, dx=-1)
+                store(True, 0, q)
                 store(True, 1, q)
-            for q in range(2):
-                come(False, 2, 3, q)
+            for q in range(len(SPLIT)):
+                come(False, 2, 3, q, 0)
+                come(False, 2, 7, q, 1)
                 store(False, 2, q)
                 come(True, -1, 5, q)
                 store(True, -1, q)
-            for q in range(2):
+            for q in range(len(SPLIT)):
                 come(True, 2, 6, q)
                 store(True, 2, q)
             for st in stores:
                 st.wait()
         for cp in cps:
             cp.wait_send()
+
+
+def hand_on(refined, logs, refined_out, logs_out, held, held_logs, sems):
+    parts = [(logs, held_logs, logs_out)]
+    parts += [(refined.at[k], held.at[k], refined_out.at[k]) for k in range(2 * NX)]
+    into = [pltpu.make_async_copy(a, b, sems.at[0, k]) for k, (a, b, _) in enumerate(parts)]
+    back = [pltpu.make_async_copy(b, o, sems.at[1, k]) for k, (_, b, o) in enumerate(parts)]
+    for cp in into:
+        cp.start()
+    for i, o in zip(into, back):
+        i.wait()
+        o.start()
+    for cp in back:
+        cp.wait()
 
 
 def on_device(minibatch, centroids):
@@ -418,11 +449,11 @@
             dma((ITERS, NY, NC)), dma((ITERS, NY, NC)),
             dma((ITERS, NZ)), dma((ITERS, NZ)),
             dma((ITERS,)), dma((ITERS,)),
-            dma((ITERS, 2, NX)), dma((ITERS, 2, NX)),
+            dma((ITERS, len(SPLIT), NX)), dma((ITERS, len(SPLIT), NX)),
             dma((ITERS, NX)), dma((ITERS, NX)),
-            dma((2, NX)), dma((2, NX)),
-            dma((2, 7)), dma((2, 7)),
-            dma(()), dma((16,)),
+            dma((len(SPLIT), NX)), dma((len(SPLIT), NX)),
+            dma((len(SPLIT), 8)), dma((len(SPLIT), 8)),
+            dma(()), dma((8 * len(SPLIT),)),
         ],
         compiler_params=pltpu.CompilerParams(
             collective_id=0, has_side_effects=True, vmem_limit_bytes=56 * 2**20
@@ -430,7 +461,20 @@
         cost_estimate=pl.CostEstimate(flops=12884901888, bytes_accessed=8 * 2**20, transcendentals=4194304),
         name="em",
     )(minibatch, centroids)
-    return (refined.reshape(2 * NX * KC, D), logs.reshape(NZ * CHUNK))
+    n = 2 * NX
+    refined, logs = pl.pallas_call(
+        hand_on,
+        out_shape=(jax.ShapeDtypeStruct((n, KC, D), F32), jax.ShapeDtypeStruct((2 * NZ, 128), F32)),
+        in_specs=[pl.BlockSpec(memory_space=pl.ANY)] * 2,
+        out_specs=[pl.BlockSpec(memory_space=pl.ANY)] * 2,
+        scratch_shapes=[
+            pltpu.VMEM((n, KC, D), F32),
+            pltpu.VMEM((2 * NZ, 128), F32),
+            dma((2, n + 1)),
+        ],
+        name="hand_on",
+    )(refined.reshape(n, KC, D), logs)
+    return (refined.reshape(n * KC, D), logs.reshape(NZ * CHUNK))
 
 
 def solution(mesh):

time: 120 us -> 113 us (0.942)
  local copies, waits for them, and re-layouts: 4.36 us -> 0 us
  Pallas kernels: 115 us -> 111 us
    pallas_call x1, Pallas kernels: 115 us -> 109 us  [on_device(): pl.pallas_call(body, out_shape=(jax.ShapeDtypeStruct((2, NX, KC, D), F32)...]
    unnamed x4 -> x0, local copies, waits for them, and re-layouts: 4.36 us -> none
    pallas_call x0 -> x1, Pallas kernels: none -> 2.82 us  [on_device(): pl.pallas_call(hand_on, out_shape=(jax.ShapeDtypeStruct((n, KC, D), F32),...]
where the time goes in v3:
time: 113 us; the launch traced here: 112 us
  Pallas kernels  111 us (98%)
    pallas_call x1, Pallas kernels, on_device(): pl.pallas_call(body, out_shape=(jax.ShapeDtypeStruct((2, NX, KC, D), F32)...  109 us
    pallas_call x1, Pallas kernels, on_device(): pl.pallas_call(hand_on, out_shape=(jax.ShapeDtypeStruct((n, KC, D), F32),...  2.82 us

profile of v3, /device:TPU:2, one launch (start us, length us, event | category | flops | bytes accessed | tf_op | source)
XLA Modules:
  0.0 112.3 jit_solution(6599668372256618262)
XLA Ops:
  0.6 108.7 %em.1 = (f32[2,4,128,768]{3,2,1,0:T(8,128)}, f32[16,128]{1,0:T(8,128)}) custom-call(bf16[64,768]{1,0:T(8,128)(2,1)} %mb.1, f32[1024,768]{1,0:T(8,128)} %cents.1), custom_call_target="tpu_custom_call" | custom-call | flops 12884901888 | bytes 8388608 | tf_op jit(solution)/shard_map/em/pallas_call | solution.py:419
  109.3 2.8 %hand_on.1 = (f32[8,128,768]{2,1,0:T(8,128)}, f32[16,128]{1,0:T(8,128)}) custom-call(f32[8,128,768]{2,1,0:T(8,128)} %bitcast.3, f32[16,128]{1,0:T(8,128)} %get-tuple-element.7.logs), custom_call_target="tpu_custom_call" | custom-call | tf_op jit(solution)/shard_map/hand_on/pallas_call | solution.py:465

commit v4 on v3

--- a/solution.py
+++ b/solution.py
@@ -19,7 +19,8 @@
 CHUNK = 256
 SC = 512
 ROWS = NZ * SC
-SPLIT = ((0, 512), (512, 256))
+SLOT = {0: 0, 1: 1, 3: 2, 2: 3}
+SPLIT = ((0, 384), (384, 384))
 KC = 128
 KD = NX * KC
 D = 768
@@ -195,7 +196,7 @@
             for d in range(NX):
                 first = pl.multiple_of(lax.rem(x + NX - d, NX) * KC, KC)
                 v = unit(cen_in[pl.ds(first, KC)])
-                cb[0, d] = v.astype(BF)
+                cb[0, SLOT[d]] = v.astype(BF)
                 if d == 0:
                     c_own[...] = v
         score_group(stage - 2)
@@ -225,8 +226,12 @@
                 score(zz, pl.ds(0, KC), cb[it, 0], True)
                 return carry
 
-            def others(zz, carry):
-                score(zz, pl.ds(KC, KD - KC), cb[it, 1:].reshape(KD - KC, D), False)
+            def near(zz, carry):
+                score(zz, pl.ds(KC, 2 * KC), cb[it, 1:3].reshape(2 * KC, D), False)
+                return carry
+
+            def far(zz, carry):
+                score(zz, pl.ds(3 * KC, KC), cb[it, 3], False)
                 return carry
 
             lax.fori_loop(0, NZ, own, 0, unroll=4)
@@ -234,16 +239,17 @@
             for q, (lo, n) in enumerate(SPLIT):
                 cols = pl.ds(lo, n)
                 for d, k, half in ((1, 2, 0), (3, 0, 1)):
-                    b = cb.at[it, d, :, cols]
+                    b = cb.at[it, SLOT[d], :, cols]
                     copy(b, b, ag_s.at[q, d], ag_r.at[q, d], dev(dx=d)).wait_recv()
                     part = pl.ds(half * KC // 2, KC // 2)
-                    src, dst = cb.at[it, d, part, cols], cb.at[it, 2, part, cols]
+                    src, dst = cb.at[it, SLOT[d], part, cols], cb.at[it, SLOT[2], part, cols]
                     relays.append(copy(src, dst, ag_s.at[q, k], ag_r.at[q, k], dev(dx=d)))
                     relays[-1].start()
+            lax.fori_loop(0, NZ, near, 0, unroll=4)
             for r in relays:
                 r.wait_recv()
             cps += relays
-            lax.fori_loop(0, NZ, others, 0, unroll=4)
+            lax.fori_loop(0, NZ, far, 0, unroll=4)
 
         ar_b[it, y, c] = tp[c]
         for d, e in ((2, 0), (2, 1), (1, 0), (3, 0), (1, 1), (3, 1), (0, 1)):
@@ -276,7 +282,7 @@
         cps.append(back)
 
         def block_of(d):
-            return pl.ds((NX - d) % NX * KC, KC)
+            return pl.ds(SLOT[(NX - d) % NX] * KC, KC)
 
         for q, (lo, n) in enumerate(SPLIT):
             cols = pl.ds(lo, n)
@@ -356,7 +362,7 @@
                 cb[it + 1, 0, :, cols] = new.astype(BF)
                 for d in (1, 3):
                     b = cb.at[it + 1, 0, :, cols]
-                    cps.append(copy(b, cb.at[it + 1, d, :, cols], ag_s.at[q, d], ag_r.at[q, d], dev(dx=d)))
+                    cps.append(copy(b, cb.at[it + 1, SLOT[d], :, cols], ag_s.at[q, d], ag_r.at[q, d], dev(dx=d)))
                     cps[-1].start()
             else:
                 coded[slot(False, 0, q)] = encode(new)

time: 113 us -> 111 us (0.982)
    pallas_call x1, Pallas kernels: 109 us -> 108 us  [on_device(): pl.pallas_call(body, out_shape=(jax.ShapeDtypeStruct((2, NX, KC, D), F32)...]
where the time goes in v4:
time: 111 us
  Pallas kernels  110 us (99%)
    pallas_call x1, Pallas kernels, on_device(): pl.pallas_call(body, out_shape=(jax.ShapeDtypeStruct((2, NX, KC, D), F32)...  108 us
    pallas_call x1, Pallas kernels, on_device(): pl.pallas_call(hand_on, out_shape=(jax.ShapeDtypeStruct((n, KC, D), F32),...  2.82 us

profile of v4, /device:TPU:2, one launch (start us, length us, event | category | flops | bytes accessed | tf_op | source)
XLA Modules:
  0.0 111.2 jit_solution(15305792982736365494)
XLA Ops:
  0.6 107.5 %em.1 = (f32[2,4,128,768]{3,2,1,0:T(8,128)}, f32[16,128]{1,0:T(8,128)}) custom-call(bf16[64,768]{1,0:T(8,128)(2,1)} %mb.1, f32[1024,768]{1,0:T(8,128)} %cents.1), custom_call_target="tpu_custom_call" | custom-call | flops 12884901888 | bytes 8388608 | tf_op jit(solution)/shard_map/em/pallas_call | solution.py:425
  108.2 2.8 %hand_on.1 = (f32[8,128,768]{2,1,0:T(8,128)}, f32[16,128]{1,0:T(8,128)}) custom-call(f32[8,128,768]{2,1,0:T(8,128)} %bitcast.3, f32[16,128]{1,0:T(8,128)} %get-tuple-element.7.logs), custom_call_target="tpu_custom_call" | custom-call | tf_op jit(solution)/shard_map/hand_on/pallas_call | solution.py:471

commit v5 on v4

--- a/solution.py
+++ b/solution.py
@@ -406,17 +406,12 @@
             cp.wait_send()
 
 
-def hand_on(refined, logs, refined_out, logs_out, held, held_logs, sems):
-    parts = [(logs, held_logs, logs_out)]
-    parts += [(refined.at[k], held.at[k], refined_out.at[k]) for k in range(2 * NX)]
-    into = [pltpu.make_async_copy(a, b, sems.at[0, k]) for k, (a, b, _) in enumerate(parts)]
-    back = [pltpu.make_async_copy(b, o, sems.at[1, k]) for k, (_, b, o) in enumerate(parts)]
-    for cp in into:
+def hand_on(refined, logs, refined_out, logs_out, sems):
+    parts = [(logs, logs_out)] + [(refined.at[k], refined_out.at[k]) for k in range(2 * NX)]
+    copies = [pltpu.make_async_copy(a, b, sems.at[k]) for k, (a, b) in enumerate(parts)]
+    for cp in copies:
         cp.start()
-    for i, o in zip(into, back):
-        i.wait()
-        o.start()
-    for cp in back:
+    for cp in copies:
         cp.wait()
 
 
@@ -462,7 +457,7 @@
             dma(()), dma((8 * len(SPLIT),)),
         ],
         compiler_params=pltpu.CompilerParams(
-            collective_id=0, has_side_effects=True, vmem_limit_bytes=56 * 2**20
+            collective_id=0, has_side_effects=True, vmem_limit_bytes=40 * 2**20
         ),
         cost_estimate=pl.CostEstimate(flops=12884901888, bytes_accessed=8 * 2**20, transcendentals=4194304),
         name="em",
@@ -473,11 +468,8 @@
         out_shape=(jax.ShapeDtypeStruct((n, KC, D), F32), jax.ShapeDtypeStruct((2 * NZ, 128), F32)),
         in_specs=[pl.BlockSpec(memory_space=pl.ANY)] * 2,
         out_specs=[pl.BlockSpec(memory_space=pl.ANY)] * 2,
-        scratch_shapes=[
-            pltpu.VMEM((n, KC, D), F32),
-            pltpu.VMEM((2 * NZ, 128), F32),
-            dma((2, n + 1)),
-        ],
+        scratch_shapes=[dma((n + 1,))],
+        compiler_params=pltpu.CompilerParams(vmem_limit_bytes=8 * 2**20),
         name="hand_on",
     )(refined.reshape(n, KC, D), logs)
     return (refined.reshape(n * KC, D), logs.reshape(NZ * CHUNK))

time: 111 us -> 111 us (level)
  Pallas kernels: 110 us -> 107 us
  local copies, waits for them, and re-layouts: 0 us -> 2.77 us
    unnamed x0 -> x4, local copies, waits for them, and re-layouts: none -> 2.77 us
    pallas_call x1, Pallas kernels: 108 us -> 105 us  [on_device(): pl.pallas_call(body, out_shape=(jax.ShapeDtypeStruct((2, NX, KC, D), F32)...]
where the time goes in v5:
time: 111 us
  Pallas kernels  107 us (96%)
  local copies, waits for them, and re-layouts  2.77 us (2%)
    pallas_call x1, Pallas kernels, on_device(): pl.pallas_call(body, out_shape=(jax.ShapeDtypeStruct((2, NX, KC, D), F32)...  105 us
    unnamed x4, local copies, waits for them, and re-layouts  2.77 us

profile of v5, /device:TPU:2, one launch (start us, length us, event | category | flops | bytes accessed | tf_op | source)
XLA Modules:
  0.0 110.6 jit_solution(10114591882849536563)
XLA Ops:
  0.6 0.0 copy-start
  0.6 1.9 %copy-done = f32[1024,768]{1,0:T(8,128)S(1)} copy-done((f32[1024,768]{1,0:T(8,128)S(1)}, f32[1024,768]{1,0:T(8,128)}, u32[]{:S(2)}) %copy-start) | copy-done | bytes 3145752
  2.5 0.0 copy-start.1
  2.5 0.9 copy-done.1
  3.4 105.3 %em.1 = (f32[2,4,128,768]{3,2,1,0:T(8,128)S(1)}, f32[16,128]{1,0:T(8,128)S(1)}) custom-call(bf16[64,768]{1,0:T(8,128)(2,1)S(1)} %copy-done.1, f32[1024,768]{1,0:T(8,128)S(1)} %copy-done), custom_call_target="tpu_custom_call" | custom-call | flops 12884901888 | bytes 8388608 | tf_op jit(solution)/shard_map/em/pallas_call | solution.py:420
  108.7 1.7 %hand_on.1 = (f32[8,128,768]{2,1,0:T(8,128)}, f32[16,128]{1,0:T(8,128)}) custom-call(f32[8,128,768]{2,1,0:T(8,128)S(1)} %bitcast.3, f32[16,128]{1,0:T(8,128)S(1)} %get-tuple-element.7.logs), custom_call_target="tpu_custom_call" | custom-call | tf_op jit(solution)/shard_map/hand_on/pallas_call | solution.py:466
Async XLA Ops:
  0.6 1.9 %copy-start = (f32[1024,768]{1,0:T(8,128)S(1)}, f32[1024,768]{1,0:T(8,128)}, u32[]{:S(2)}) copy-start(f32[1024,768]{1,0:T(8,128)} %cents.1) | copy-start | bytes 9437188
  2.5 0.9 copy-start.1
